TPU v7x, 512 devices: a whole 4x4x16 slice. The times are simulated.
512 devices in a mesh: visit: 32 (over z, x_lo), patch: 16 (over x_hi, y, core).
Axes of the slice: x: 4 (x_hi: 2, x_lo: 2; x = x_hi * 2 + x_lo), y: 4, z: 16, core: 2. Of those that a mesh axis runs over, the one named last changes fastest.
Arguments:
- templates: float32 [32, 2, 256, 1024], P('visit', None, 'patch'), may hold values from -16 to 16, as said below
- owners: int32 [2], replicated, may hold values from 0 to 31, as said below
- science: float32 [2, 32, 256, 1024], P(None, 'visit', 'patch'), may hold values from -40 to 40
- sci_var: float32 [2, 32, 256, 1024], P(None, 'visit', 'patch'), may hold values from 0.03 to 0.3
- bad_pixels: int32 [2, 32, 256, 1024], P(None, 'visit', 'patch'), may hold values 0 or 1
Outputs:
- significance: float32 [2, 32, 256, 1024], P(None, 'visit', 'patch')
Inputs may be any that keep to these rules, and one draw needn't show every extreme that they name: `owners`: the steps' entries are distinct indices of stored tiles, one of them always 32 - 1. `templates`: variances (index 1) lie in 0.01 to 0.1.
All inputs are finite; a program needn't handle non-finite values. No bound on the sum of `bad_pixels` on one device may be relied on, other than what follows from the above.
Results may differ from a plain program's by a relative error of at most 0.0003.
Values sent between devices are 32-bit elements; how exact they have to be, the bound alone decides.
A program may use at most 64 MiB of HBM per device.

v0:
```python
import jax
import jax.numpy as jnp
import numpy as np
from jax import lax
from jax.sharding import PartitionSpec as P

NPROF = 5
RAD = 10
STEPS = 2
ridge = 1.0


def from_root(block, axis, holder):
    block = jnp.where(lax.axis_index(axis) == holder, block, jnp.zeros_like(block))
    return lax.psum(block, axis)


def padded(cells, sides, width):
    for axis, dim in sides:
        count = lax.axis_size(axis)
        ends = count - 1
        head = lax.slice_in_dim(cells, 0, width, axis=dim)
        tail = lax.slice_in_dim(cells, cells.shape[dim] - width, cells.shape[dim], axis=dim)
        cells = jnp.concatenate(
            [
                lax.ppermute(tail, axis, [(i, (i + 1) % count) for i in range(ends)]),
                cells,
                lax.ppermute(head, axis, [((i + 1) % count, i) for i in range(ends)]),
            ],
            axis=dim,
        )
    return cells


def profile_table():
    offsets = np.arange(-RAD, RAD + 1) * 1.0
    recipe = [(1.0, 0), (1.5, 1), (2.0, 2), (3.0, 0), (4.0, 1)]
    profiles = []
    for spread, degree in recipe[:NPROF]:
        profile = offsets**degree * np.exp(-offsets * offsets / (2.0 * spread * spread))
        for earlier in profiles:
            profile = profile - np.dot(earlier, profile) * earlier
        profile = profile / np.sqrt(np.dot(profile, profile))
        profiles.append(profile)
    return np.stack(profiles)


def band_table(profiles, outputs, inputs):
    distance = jnp.arange(inputs)[None, :] - jnp.arange(outputs)[:, None]
    table = jnp.zeros((NPROF, outputs, inputs), jnp.float32)
    for offset in range(2 * RAD + 1):
        table = (
            table + profiles[:, offset, None, None] * (distance == offset).astype(jnp.float32)[None]
        )
    return table


def basis_images(extended):
    profiles = jnp.asarray(profile_table(), jnp.float32)
    height = extended.shape[0] - 2 * RAD
    across = extended.shape[1]
    block_width = 128
    block_count = across // block_width
    widened = jnp.pad(extended, ((0, 0), (RAD, RAD)))
    blocks = jnp.stack(
        [
            widened[:, start * block_width : start * block_width + block_width + 2 * RAD]
            for start in range(block_count)
        ]
    )
    col_table = jnp.transpose(band_table(profiles, block_width, block_width + 2 * RAD), (0, 2, 1))
    columns = jnp.einsum("srx,kxc->krsc", blocks, col_table, precision=lax.Precision.HIGHEST)
    columns = columns.reshape(NPROF, extended.shape[0], across)
    row_table = band_table(profiles, height, height + 2 * RAD)
    images = jnp.einsum("lhr,krc->klhc", row_table, columns, precision=lax.Precision.HIGHEST)
    return images.reshape(NPROF * NPROF, height, across)


def solve_kernel(normal_mat, normal_rhs):
    count = normal_mat.shape[0]
    factor = jnp.linalg.cholesky(normal_mat + ridge * jnp.eye(count, dtype=jnp.float32))
    return jax.scipy.linalg.cho_solve((factor, True), normal_rhs)


def finish_step(normal_mat, normal_rhs, flattened, usable, noise_var, image_sci):
    kernel_coef = jax.vmap(solve_kernel)(normal_mat, normal_rhs)
    fitted = jnp.einsum(
        "vb,bp->vp", kernel_coef, flattened, precision=lax.Precision.HIGHEST
    ).reshape(image_sci.shape)
    return usable * (image_sci - fitted) / jnp.sqrt(noise_var)


def shards(templates, owners, science, sci_var, bad_pixels):
    own_pair = templates[0]
    visit_count = science.shape[1]
    basis_count = NPROF * NPROF
    results = []
    for current in range(STEPS):
        owner_index = owners[current]
        arrived = from_root(own_pair, "visit", owner_index)
        extended = padded(arrived[0], (("patch", 0),), RAD)
        tile_var = arrived[1]
        images = basis_images(extended)
        flattened = images.reshape(basis_count, -1)
        usable = (1 - bad_pixels[current]).astype(jnp.float32)
        noise_var = sci_var[current] + tile_var[None]
        weight = usable / noise_var
        weighted = (images[None] * weight[:, None]).reshape(visit_count, basis_count, -1)
        normal_mat = jnp.einsum("vbp,cp->vbc", weighted, flattened, precision=lax.Precision.HIGHEST)
        normal_rhs = jnp.einsum(
            "cp,vp->vc",
            flattened,
            (weight * science[current]).reshape(visit_count, -1),
            precision=lax.Precision.HIGHEST,
        )
        summed_mat, summed_rhs = lax.psum((normal_mat, normal_rhs), "patch")
        results.append(
            finish_step(summed_mat, summed_rhs, flattened, usable, noise_var, science[current])
        )
    return jnp.stack(results)


def solution(mesh):
    return jax.shard_map(
        shards,
        mesh=mesh,
        in_specs=(
            P("visit", None, "patch", None),
            P(),
            P(None, "visit", "patch", None),
            P(None, "visit", "patch", None),
            P(None, "visit", "patch", None),
        ),
        out_specs=P(None, "visit", "patch", None),
        check_vma=False,
    )
```

profile of v0, /device:TPU:4, one launch (start us, length us, event | category | flops | bytes accessed | tf_op | source)
XLA Modules:
  0.0 429.1 jit_solution(2009927834076208268)
XLA Ops:
  6.8 1.4 fusion.136
  9.5 1.6 select_bitcast_fusion.1
  12.7 263.9 %all-reduce.6.cloned.1.call-done = (f32[2,16,1024]{2,1,0:T(8,128)}, f32[2,16,1024]{2,1,0:T(8,128)}) async-done(((f32[2,16,1024]{2,1,0:T(8,128)}, f32[2,16,1024]{2,1,0:T(8,128)}), (f32[2,16,1024]{2,1,0:T(8,128)}, f32[2,16,1024]{2,1,0:T(8,128)})) %all-reduce.6.cloned.1.call-update) | async-done | bytes 262160 | tf_op jit(solution)/shard_map/psum | solution.py:15
  277.5 1.9 collective-permute-start.2
  279.5 7.3 %collective-permute-start.3 = (f32[10,1024]{1,0:T(8,128)S(1)}, f32[10,1024]{1,0:T(8,128)S(1)}, u32[]{:S(2)}, u32[]{:S(2)}) collective-permute-start(f32[10,1024]{1,0:T(8,128)S(1)} %get-tuple-element.24), channel_id=1, source_target_pairs={{1,0},{2,1},{3,2},{4,3},{5,4},{6,5},{7,6},{8,7},{9,8},{10,9},{11,1... | collective-permute-start | bytes 122888 | tf_op jit(solution)/shard_map/ppermute | solution.py:28
  287.6 1.9 collective-permute-start
  289.6 7.3 %collective-permute-start.1 = (f32[10,1024]{1,0:T(8,128)S(1)}, f32[10,1024]{1,0:T(8,128)S(1)}, u32[]{:S(2)}, u32[]{:S(2)}) collective-permute-start(f32[10,1024]{1,0:T(8,128)S(1)} %get-tuple-element.22), channel_id=1, source_target_pairs={{1,0},{2,1},{3,2},{4,3},{5,4},{6,5},{7,6},{8,7},{9,8},{10,9},{11,1... | collective-permute-start | bytes 122888 | tf_op jit(solution)/shard_map/ppermute | solution.py:28
  303.1 1.6 bitcast_multiply_fusion.1
  305.0 1.6 bitcast_multiply_fusion
  309.7 1.8 convolution_bitcast_fusion.3
  311.6 2.5 fusion.137
  316.8 2.4 convolution_bitcast_fusion.2
  319.3 2.3 fusion.138
  321.6 70.9 %all-reduce.3 = (f32[1,25,25]{1,2,0:T(8,128)}, f32[1,25]{1,0:T(1,128)}, f32[1,25,25]{1,2,0:T(8,128)}, f32[1,25]{1,0:T(1,128)}) all-reduce(f32[1,25,25]{1,2,0:T(8,128)} %convolution_bitcast_fusion.2, f32[1,25]{1,0:T(1,128)} %fusion.138, ...), channel_id=1, replica_groups=mesh['visit'=32,'patch'=16] {'patch'}, use_global_device_ids=true, to_apply=%region_6.9 | all-reduce | flops 1300 | bytes 10400 | tf_op jit(solution)/shard_map/psum | solution.py:116
  392.5 1.3 convert_add_fusion
  394.6 1.3 fusion.86
  396.0 3.0 custom-call.12
  400.8 2.6 custom-call.13
  404.9 1.3 convert_add_fusion.1
  407.0 1.3 fusion.89
  408.3 3.0 custom-call.10
  413.3 2.6 custom-call.11
  416.9 2.6 fusion
  419.5 2.0 fusion.2
  (140 shorter events, 24.1 us)
Async XLA Ops:
  6.5 5.0 %copy-start.9 = (f32[5]{0:T(128)S(1)}, f32[5]{0:T(128)}, u32[]{:S(2)}) copy-start(f32[5]{0:T(128)} %constant.161) | copy-start | bytes 64
  6.5 5.0 %copy-start.10 = (f32[5]{0:T(128)S(1)}, f32[5]{0:T(128)}, u32[]{:S(2)}) copy-start(f32[5]{0:T(128)} %constant.159) | copy-start | bytes 64
  6.5 5.1 %copy-start.11 = (f32[5]{0:T(128)S(1)}, f32[5]{0:T(128)}, u32[]{:S(2)}) copy-start(f32[5]{0:T(128)} %constant.157) | copy-start | bytes 64
  6.5 5.1 %copy-start.12 = (f32[5]{0:T(128)S(1)}, f32[5]{0:T(128)}, u32[]{:S(2)}) copy-start(f32[5]{0:T(128)} %constant.155) | copy-start | bytes 64
  6.6 5.1 %copy-start.13 = (f32[5]{0:T(128)S(1)}, f32[5]{0:T(128)}, u32[]{:S(2)}) copy-start(f32[5]{0:T(128)} %constant.153) | copy-start | bytes 64
  6.6 5.1 %copy-start.14 = (f32[5]{0:T(128)S(1)}, f32[5]{0:T(128)}, u32[]{:S(2)}) copy-start(f32[5]{0:T(128)} %constant.151) | copy-start | bytes 64
  6.6 5.1 %copy-start.15 = (f32[5]{0:T(128)S(1)}, f32[5]{0:T(128)}, u32[]{:S(2)}) copy-start(f32[5]{0:T(128)} %constant.149) | copy-start | bytes 64
  6.6 5.1 %copy-start.16 = (f32[5]{0:T(128)S(1)}, f32[5]{0:T(128)}, u32[]{:S(2)}) copy-start(f32[5]{0:T(128)} %constant.147) | copy-start | bytes 64
  6.6 5.1 %copy-start.17 = (f32[5]{0:T(128)S(1)}, f32[5]{0:T(128)}, u32[]{:S(2)}) copy-start(f32[5]{0:T(128)} %constant.145) | copy-start | bytes 64
  6.6 5.1 %copy-start.18 = (f32[5]{0:T(128)S(1)}, f32[5]{0:T(128)}, u32[]{:S(2)}) copy-start(f32[5]{0:T(128)} %constant.143) | copy-start | bytes 64
  6.6 5.1 %copy-start.19 = (f32[5]{0:T(128)S(1)}, f32[5]{0:T(128)}, u32[]{:S(2)}) copy-start(f32[5]{0:T(128)} %constant.141) | copy-start | bytes 64
  6.6 5.0 %copy-start.20 = (f32[5]{0:T(128)S(1)}, f32[5]{0:T(128)}, u32[]{:S(2)}) copy-start(f32[5]{0:T(128)} %constant.139) | copy-start | bytes 64
  6.7 5.0 %copy-start.21 = (f32[5]{0:T(128)S(1)}, f32[5]{0:T(128)}, u32[]{:S(2)}) copy-start(f32[5]{0:T(128)} %constant.137) | copy-start | bytes 64
  6.7 5.0 %copy-start.22 = (f32[5]{0:T(128)S(1)}, f32[5]{0:T(128)}, u32[]{:S(2)}) copy-start(f32[5]{0:T(128)} %constant.135) | copy-start | bytes 64
  6.7 5.0 %copy-start.23 = (f32[5]{0:T(128)S(1)}, f32[5]{0:T(128)}, u32[]{:S(2)}) copy-start(f32[5]{0:T(128)} %constant.133) | copy-start | bytes 64
  6.7 5.0 %copy-start.24 = (f32[5]{0:T(128)S(1)}, f32[5]{0:T(128)}, u32[]{:S(2)}) copy-start(f32[5]{0:T(128)} %constant.131) | copy-start | bytes 64
  6.8 269.8 %all-reduce.6.cloned.1.call-start = ((), (), s32[]{:S(2)}) async-start(), calls=%async_computation | async-start | bytes 524288 | tf_op jit(solution)/shard_map/psum | solution.py:15
  11.3 285.5 %copy-start.2 = (f32[2,1,16,1024]{3,2,1,0:T(8,128)S(1)}, f32[2,1,16,1024]{3,2,1,0:T(8,128)}, u32[]{:S(2)}) copy-start(f32[2,1,16,1024]{3,2,1,0:T(8,128)} %param.12) | copy-start | bytes 393220
  11.3 285.5 %copy-start.3 = (f32[2,1,16,1024]{3,2,1,0:T(8,128)S(1)}, f32[2,1,16,1024]{3,2,1,0:T(8,128)}, u32[]{:S(2)}) copy-start(f32[2,1,16,1024]{3,2,1,0:T(8,128)} %param.13) | copy-start | bytes 393220
  11.3 285.5 %copy-start.4 = (s32[2,1,16,1024]{3,2,1,0:T(8,128)S(1)}, s32[2,1,16,1024]{3,2,1,0:T(8,128)}, u32[]{:S(2)}) copy-start(s32[2,1,16,1024]{3,2,1,0:T(8,128)} %param.14) | copy-start | bytes 393220
  277.5 21.7 %collective-permute-start.2 = (f32[10,1024]{1,0:T(8,128)S(1)}, f32[10,1024]{1,0:T(8,128)S(1)}, u32[]{:S(2)}, u32[]{:S(2)}) collective-permute-start(f32[10,1024]{1,0:T(8,128)S(1)} %get-tuple-element.23), channel_id=1, source_target_pairs={{0,1},{1,2},{2,3},{3,4},{4,5},{5,6},{6,7},{7,8},{8,9},{9,10},{10,1... | collective-permute-start | bytes 122888 | tf_op jit(solution)/shard_map/ppermute | solution.py:26
  279.5 19.8 %collective-permute-start.3 = (f32[10,1024]{1,0:T(8,128)S(1)}, f32[10,1024]{1,0:T(8,128)S(1)}, u32[]{:S(2)}, u32[]{:S(2)}) collective-permute-start(f32[10,1024]{1,0:T(8,128)S(1)} %get-tuple-element.24), channel_id=1, source_target_pairs={{1,0},{2,1},{3,2},{4,3},{5,4},{6,5},{7,6},{8,7},{9,8},{10,9},{11,1... | collective-permute-start | bytes 122888 | tf_op jit(solution)/shard_map/ppermute | solution.py:28
  287.6 11.6 %collective-permute-start = (f32[10,1024]{1,0:T(8,128)S(1)}, f32[10,1024]{1,0:T(8,128)S(1)}, u32[]{:S(2)}, u32[]{:S(2)}) collective-permute-start(f32[10,1024]{1,0:T(8,128)S(1)} %get-tuple-element.21), channel_id=1, source_target_pairs={{0,1},{1,2},{2,3},{3,4},{4,5},{5,6},{6,7},{7,8},{8,9},{9,10},{10,1... | collective-permute-start | bytes 122888 | tf_op jit(solution)/shard_map/ppermute | solution.py:26
  289.6 9.7 %collective-permute-start.1 = (f32[10,1024]{1,0:T(8,128)S(1)}, f32[10,1024]{1,0:T(8,128)S(1)}, u32[]{:S(2)}, u32[]{:S(2)}) collective-permute-start(f32[10,1024]{1,0:T(8,128)S(1)} %get-tuple-element.22), channel_id=1, source_target_pairs={{1,0},{2,1},{3,2},{4,3},{5,4},{6,5},{7,6},{8,7},{9,8},{10,9},{11,1... | collective-permute-start | bytes 122888 | tf_op jit(solution)/shard_map/ppermute | solution.py:28
  (10 other events, 43.4 us)
Sparse Core Ops, SparseCore 0:
  11.2 265.3 all-reduce.5
where the time goes:
time: 430 us; the launch traced here: 429 us
  waiting for transfers between devices  264 us (61%)
  blocking collectives  70.9 us (16%)
  other arithmetic  24.9 us (6%)
  matrix products  21.2 us (5%)
  starting transfers between devices  18.4 us (4%)
  between operations  15.5 us (4%)
  local copies, waits for them, and re-layouts  14.3 us (3%)
    psum x1, waiting for transfers between devices, from_root(): return lax.psum(block, axis)  264 us
    psum x1, blocking collectives, shards(): summed_mat, summed_rhs = lax.psum((normal_mat, normal_rhs), 'patch')  70.9 us
    ppermute x2, starting transfers between devices, padded(): lax.ppermute(head, axis, [((i + 1) % count, i) for i in range(ends)])  14.5 us
  transfers between devices with their start and end apart: 5, of which 1 were waited for; matrix products, arithmetic and copies ran while one was open for 1% of the time, Pallas kernels for 0%

commit v1 on v0

--- a/solution.py
+++ b/solution.py
@@ -12,7 +12,7 @@
 
 def from_root(block, axis, holder):
     block = jnp.where(lax.axis_index(axis) == holder, block, jnp.zeros_like(block))
-    return lax.psum(block, axis)
+    return jnp.sum(lax.all_gather(block, axis), axis=0)
 
 
 def padded(cells, sides, width):

time: 430 us -> 447 us (1.040)
  waiting for transfers between devices: 264 us -> 272 us
  other arithmetic: 24.9 us -> 29.5 us
    all_gather x0 -> x2, waiting for transfers between devices: none -> 271 us  [from_root(): return jnp.sum(lax.all_gather(block, axis), axis=0)]
    psum x1 -> x0, waiting for transfers between devices: 264 us -> none  [from_root(): return lax.psum(block, axis)]
    reduce_sum x0 -> x2, other arithmetic: none -> 4.86 us  [from_root(): return jnp.sum(lax.all_gather(block, axis), axis=0)]
    unnamed x82 -> x86, local copies, waits for them, and re-layouts: 8.57 us -> 11.6 us
  transfers between devices with their start and end apart: 5 -> 6, of which waited for: 1 -> 2; matrix products, arithmetic and copies ran while one was open for 1% -> 2% of each run, Pallas kernels for 0% -> 0%
where the time goes in v1:
time: 447 us; the launch traced here: 445 us
  waiting for transfers between devices  272 us (61%)
  blocking collectives  71 us (16%)
  other arithmetic  29.5 us (7%)
  matrix products  23.2 us (5%)
  starting transfers between devices  18.7 us (4%)
  local copies, waits for them, and re-layouts  15.5 us (3%)
  between operations  15.5 us (3%)
    all_gather x2, waiting for transfers between devices, from_root(): return jnp.sum(lax.all_gather(block, axis), axis=0)  271 us
    psum x1, blocking collectives, shards(): summed_mat, summed_rhs = lax.psum((normal_mat, normal_rhs), 'patch')  71 us
    ppermute x2, starting transfers between devices, padded(): lax.ppermute(head, axis, [((i + 1) % count, i) for i in range(ends)])  14.8 us
    unnamed x86, local copies, waits for them, and re-layouts  11.6 us
  transfers between devices with their start and end apart: 6, of which 2 were waited for; matrix products, arithmetic and copies ran while one was open for 2% of the time, Pallas kernels for 0%

profile of v1, /device:TPU:4, one launch (start us, length us, event | category | flops | bytes accessed | tf_op | source)
XLA Modules:
  0.0 445.2 jit_solution(17545082469773506719)
XLA Ops:
  6.8 1.4 fusion.136
  9.5 1.6 broadcast_select_fusion.1
  13.4 143.4 %all-gather.5.cloned.1.call-done = f32[32,2,16,1024]{3,2,1,0:T(8,128)} async-done(((f32[1,2,16,1024]{3,2,1,0:T(8,128)}), f32[32,2,16,1024]{3,2,1,0:T(8,128)}) %all-gather.5.cloned.1.call-update) | async-done | bytes 4194320 | tf_op jit(solution)/shard_map/all_gather | solution.py:15
  156.8 2.4 reduce_sum.19
  159.3 1.9 collective-permute-start.2
  161.2 7.4 %collective-permute-start.3 = (f32[10,1024]{1,0:T(8,128)S(1)}, f32[10,1024]{1,0:T(8,128)S(1)}, u32[]{:S(2)}, u32[]{:S(2)}) collective-permute-start(f32[10,1024]{1,0:T(8,128)S(1)} %get-tuple-element.24), channel_id=1, source_target_pairs={{1,0},{2,1},{3,2},{4,3},{5,4},{6,5},{7,6},{8,7},{9,8},{10,9},{11,1... | collective-permute-start | bytes 122888 | tf_op jit(solution)/shard_map/ppermute | solution.py:28
  168.6 127.5 %all-gather.3.cloned.1.call-done = f32[32,2,16,1024]{3,2,1,0:T(8,128)} async-done(((f32[1,2,16,1024]{3,2,1,0:T(8,128)}), f32[32,2,16,1024]{3,2,1,0:T(8,128)}) %all-gather.3.cloned.1.call-update) | async-done | bytes 4194320 | tf_op jit(solution)/shard_map/all_gather | solution.py:15
  296.2 2.4 reduce_sum.18
  298.6 1.9 collective-permute-start
  300.5 7.4 %collective-permute-start.1 = (f32[10,1024]{1,0:T(8,128)S(1)}, f32[10,1024]{1,0:T(8,128)S(1)}, u32[]{:S(2)}, u32[]{:S(2)}) collective-permute-start(f32[10,1024]{1,0:T(8,128)S(1)} %get-tuple-element.20), channel_id=1, source_target_pairs={{1,0},{2,1},{3,2},{4,3},{5,4},{6,5},{7,6},{8,7},{9,8},{10,9},{11,1... | collective-permute-start | bytes 122888 | tf_op jit(solution)/shard_map/ppermute | solution.py:28
  312.0 2.7 bitcast_multiply_fusion.1
  314.8 1.7 pad.18
  318.4 2.5 bitcast_multiply_fusion
  325.6 1.8 convolution_bitcast_fusion.3
  327.5 2.5 fusion.137
  332.7 2.4 convolution_bitcast_fusion.2
  335.2 2.2 fusion.138
  337.4 71.0 %all-reduce.2 = (f32[1,25,25]{1,2,0:T(8,128)}, f32[1,25]{1,0:T(1,128)}, f32[1,25,25]{1,2,0:T(8,128)}, f32[1,25]{1,0:T(1,128)}) all-reduce(f32[1,25,25]{1,2,0:T(8,128)} %convolution_bitcast_fusion.2, f32[1,25]{1,0:T(1,128)} %fusion.138, ...), channel_id=1, replica_groups=mesh['visit'=32,'patch'=16] {'patch'}, use_global_device_ids=true, to_apply=%region_6.9 | all-reduce | flops 1300 | bytes 10400 | tf_op jit(solution)/shard_map/psum | solution.py:116
  411.9 3.0 custom-call.12
  416.8 2.6 custom-call.13
  424.4 3.0 custom-call.10
  429.3 2.6 custom-call.11
  432.9 2.6 fusion
  435.6 2.0 fusion.2
  (149 shorter events, 29.4 us)
Async XLA Ops:
  6.5 5.8 %copy-start.11 = (f32[5]{0:T(128)S(1)}, f32[5]{0:T(128)}, u32[]{:S(2)}) copy-start(f32[5]{0:T(128)} %constant.162) | copy-start | bytes 64
  6.5 5.8 %copy-start.12 = (f32[5]{0:T(128)S(1)}, f32[5]{0:T(128)}, u32[]{:S(2)}) copy-start(f32[5]{0:T(128)} %constant.160) | copy-start | bytes 64
  6.5 5.8 %copy-start.13 = (f32[5]{0:T(128)S(1)}, f32[5]{0:T(128)}, u32[]{:S(2)}) copy-start(f32[5]{0:T(128)} %constant.158) | copy-start | bytes 64
  6.5 5.8 %copy-start.14 = (f32[5]{0:T(128)S(1)}, f32[5]{0:T(128)}, u32[]{:S(2)}) copy-start(f32[5]{0:T(128)} %constant.156) | copy-start | bytes 64
  6.6 5.8 %copy-start.15 = (f32[5]{0:T(128)S(1)}, f32[5]{0:T(128)}, u32[]{:S(2)}) copy-start(f32[5]{0:T(128)} %constant.154) | copy-start | bytes 64
  6.6 5.8 %copy-start.16 = (f32[5]{0:T(128)S(1)}, f32[5]{0:T(128)}, u32[]{:S(2)}) copy-start(f32[5]{0:T(128)} %constant.152) | copy-start | bytes 64
  6.6 5.8 %copy-start.17 = (f32[5]{0:T(128)S(1)}, f32[5]{0:T(128)}, u32[]{:S(2)}) copy-start(f32[5]{0:T(128)} %constant.150) | copy-start | bytes 64
  6.6 5.8 %copy-start.18 = (f32[5]{0:T(128)S(1)}, f32[5]{0:T(128)}, u32[]{:S(2)}) copy-start(f32[5]{0:T(128)} %constant.148) | copy-start | bytes 64
  6.6 5.8 %copy-start.19 = (f32[5]{0:T(128)S(1)}, f32[5]{0:T(128)}, u32[]{:S(2)}) copy-start(f32[5]{0:T(128)} %constant.146) | copy-start | bytes 64
  6.6 5.8 %copy-start.20 = (f32[5]{0:T(128)S(1)}, f32[5]{0:T(128)}, u32[]{:S(2)}) copy-start(f32[5]{0:T(128)} %constant.144) | copy-start | bytes 64
  6.6 5.8 %copy-start.21 = (f32[5]{0:T(128)S(1)}, f32[5]{0:T(128)}, u32[]{:S(2)}) copy-start(f32[5]{0:T(128)} %constant.142) | copy-start | bytes 64
  6.6 5.8 %copy-start.22 = (f32[5]{0:T(128)S(1)}, f32[5]{0:T(128)}, u32[]{:S(2)}) copy-start(f32[5]{0:T(128)} %constant.140) | copy-start | bytes 64
  6.7 5.8 %copy-start.23 = (f32[5]{0:T(128)S(1)}, f32[5]{0:T(128)}, u32[]{:S(2)}) copy-start(f32[5]{0:T(128)} %constant.138) | copy-start | bytes 64
  6.7 5.8 %copy-start.24 = (f32[5]{0:T(128)S(1)}, f32[5]{0:T(128)}, u32[]{:S(2)}) copy-start(f32[5]{0:T(128)} %constant.136) | copy-start | bytes 64
  6.7 5.8 %copy-start.25 = (f32[5]{0:T(128)S(1)}, f32[5]{0:T(128)}, u32[]{:S(2)}) copy-start(f32[5]{0:T(128)} %constant.134) | copy-start | bytes 64
  6.8 150.1 %all-gather.5.cloned.1.call-start = ((), (), s32[]{:S(2)}) async-start(), calls=%async_computation.1 | async-start | bytes 4325376 | tf_op jit(solution)/shard_map/all_gather | solution.py:15
  11.1 285.0 %all-gather.3.cloned.1.call-start = ((), (), s32[]{:S(2)}) async-start(), calls=%async_computation | async-start | bytes 4325376 | tf_op jit(solution)/shard_map/all_gather | solution.py:15
  159.3 150.8 %collective-permute-start.2 = (f32[10,1024]{1,0:T(8,128)S(1)}, f32[10,1024]{1,0:T(8,128)S(1)}, u32[]{:S(2)}, u32[]{:S(2)}) collective-permute-start(f32[10,1024]{1,0:T(8,128)S(1)} %get-tuple-element.23), channel_id=1, source_target_pairs={{0,1},{1,2},{2,3},{3,4},{4,5},{5,6},{6,7},{7,8},{8,9},{9,10},{10,1... | collective-permute-start | bytes 122888 | tf_op jit(solution)/shard_map/ppermute | solution.py:26
  161.2 146.8 %copy-start.2 = (f32[2,1,16,1024]{3,2,1,0:T(8,128)S(1)}, f32[2,1,16,1024]{3,2,1,0:T(8,128)}, u32[]{:S(2)}) copy-start(f32[2,1,16,1024]{3,2,1,0:T(8,128)} %param.12) | copy-start | bytes 393220
  161.2 146.8 %copy-start.4 = (f32[2,1,16,1024]{3,2,1,0:T(8,128)S(1)}, f32[2,1,16,1024]{3,2,1,0:T(8,128)}, u32[]{:S(2)}) copy-start(f32[2,1,16,1024]{3,2,1,0:T(8,128)} %param.13) | copy-start | bytes 393220
  161.2 146.8 %copy-start.6 = (s32[2,1,16,1024]{3,2,1,0:T(8,128)S(1)}, s32[2,1,16,1024]{3,2,1,0:T(8,128)}, u32[]{:S(2)}) copy-start(s32[2,1,16,1024]{3,2,1,0:T(8,128)} %param.14) | copy-start | bytes 393220
  161.2 148.9 %collective-permute-start.3 = (f32[10,1024]{1,0:T(8,128)S(1)}, f32[10,1024]{1,0:T(8,128)S(1)}, u32[]{:S(2)}, u32[]{:S(2)}) collective-permute-start(f32[10,1024]{1,0:T(8,128)S(1)} %get-tuple-element.24), channel_id=1, source_target_pairs={{1,0},{2,1},{3,2},{4,3},{5,4},{6,5},{7,6},{8,7},{9,8},{10,9},{11,1... | collective-permute-start | bytes 122888 | tf_op jit(solution)/shard_map/ppermute | solution.py:28
  298.6 11.5 %collective-permute-start = (f32[10,1024]{1,0:T(8,128)S(1)}, f32[10,1024]{1,0:T(8,128)S(1)}, u32[]{:S(2)}, u32[]{:S(2)}) collective-permute-start(f32[10,1024]{1,0:T(8,128)S(1)} %get-tuple-element.19), channel_id=1, source_target_pairs={{0,1},{1,2},{2,3},{3,4},{4,5},{5,6},{6,7},{7,8},{8,9},{9,10},{10,1... | collective-permute-start | bytes 122888 | tf_op jit(solution)/shard_map/ppermute | solution.py:26
  300.5 9.6 %collective-permute-start.1 = (f32[10,1024]{1,0:T(8,128)S(1)}, f32[10,1024]{1,0:T(8,128)S(1)}, u32[]{:S(2)}, u32[]{:S(2)}) collective-permute-start(f32[10,1024]{1,0:T(8,128)S(1)} %get-tuple-element.20), channel_id=1, source_target_pairs={{1,0},{2,1},{3,2},{4,3},{5,4},{6,5},{7,6},{8,7},{9,8},{10,9},{11,1... | collective-permute-start | bytes 122888 | tf_op jit(solution)/shard_map/ppermute | solution.py:28
  (13 other events, 55.9 us)
Sparse Core Ops, SparseCore 0:
  11.2 145.5 all-gather.4
  158.9 137.2 all-gather.2
